TPU v7x, 32 devices: a whole 2x2x4 slice. The times are simulated.
32 devices in a mesh: parts: 2 (over y), dp: 4 (over z), mp: 2 (over x), rep: 2 (over core).
Axes of the slice: x: 2, y: 2, z: 4, core: 2. Of those that a mesh axis runs over, the one named last changes fastest.
Arguments:
- hidden_in: bfloat16 [64, 256, 1024], P(('parts', 'dp', 'rep')), parts along dimension 0, may hold values from -6 to 6
- doc_lengths: int32 [64], P(('parts', 'dp', 'rep')), parts along dimension 0, may hold values from 32 to 256
- w_qkv: bfloat16 [1024, 3, 1024], P('dp', None, 'mp'), may hold values from -6 to 6
- w_out: bfloat16 [1024, 1024], P('mp', 'dp'), may hold values from -0.1875 to 0.1875
- w_up: bfloat16 [1024, 4096], P('dp', 'mp'), may hold values from -0.1875 to 0.1875
- w_down: bfloat16 [4096, 1024], P('mp', 'dp'), may hold values from -0.09375 to 0.09375
- stored_embed: bfloat16 [2016, 1024], P(('parts', 'dp', 'mp', 'rep')), parts along dimension 0, may hold values from -6 to 6
- doc_labels: int32 [2080, 1], P(('parts', 'dp', 'mp', 'rep')), parts along dimension 0, may hold values from 0 to 3; in each aligned block of 65 rows (0 to 64, 65 to 129, ...) at most 26 rows name the same one
- doc_order: int32 [2080], P(('parts', 'dp', 'mp', 'rep')), parts along dimension 0, may hold values from 0 to 1039, each once
Outputs:
- best: float32 [2080], P(('parts', 'dp', 'mp', 'rep')), parts along dimension 0
There are 2 independent parts, one for each index of `parts`. A program takes and returns all parts, laid end to end along the dimension named above; an argument that names none is the same for every part. Nothing has to cross between parts.
Inputs may be any that keep to these rules, and one draw needn't show every extreme that they name: `doc_labels`: no label appears on more than 26 of the rows of one device. `doc_order`: every rank appears once.
All inputs are finite; a program needn't handle non-finite values.
Results may differ from a plain program's by a relative error of at most 0.005.
Values may be sent and summed in bfloat16 or wider, within the bound.
A program may use at most 64 MiB of HBM per device.

v0:
```python
import jax
import jax.numpy as jnp
from jax import lax
from jax.sharding import PartitionSpec as P

HEAD = 64
CL_OWN = 1


def normalize(values):
    centred = values - jnp.mean(values, axis=-1, keepdims=True)
    spread = jnp.mean(centred * centred, axis=-1, keepdims=True)
    return centred * lax.rsqrt(spread + 1e-05)


def unit_rows(values):
    return (values * lax.rsqrt(jnp.sum(values * values, axis=-1, keepdims=True) + 1e-06)).astype(
        jnp.bfloat16
    )


def shards(hidden_in, doc_lengths, w_qkv, w_out, w_up, w_down, stored_embed, doc_labels, doc_order):
    replica = lax.axis_index("rep")
    copies = lax.axis_size("rep")

    def rep_half(weight, along):
        extent = weight.shape[along] // copies
        return lax.dynamic_slice_in_dim(weight, replica * extent, extent, along)

    halves = (
        lax.all_gather(rep_half(w_qkv, 2), "dp", axis=0, tiled=True),
        lax.all_gather(rep_half(w_out, 0), "dp", axis=1, tiled=True),
        lax.all_gather(rep_half(w_up, 1), "dp", axis=0, tiled=True),
        lax.all_gather(rep_half(w_down, 0), "dp", axis=1, tiled=True),
    )
    qkv_full, out_full, up_full, down_full = (
        lax.all_gather(halves[0], "rep", axis=2, tiled=True),
        lax.all_gather(halves[1], "rep", axis=0, tiled=True),
        lax.all_gather(halves[2], "rep", axis=1, tiled=True),
        lax.all_gather(halves[3], "rep", axis=0, tiled=True),
    )
    doc_count, seq_len, _ = hidden_in.shape
    mp_index = lax.axis_index("mp")
    residual = hidden_in.astype(jnp.float32)
    normed = normalize(residual).astype(jnp.bfloat16)
    projected = jnp.einsum(
        "bsd,dte->bste", normed, qkv_full, preferred_element_type=jnp.float32
    ).astype(jnp.bfloat16)
    local_heads = qkv_full.shape[2] // HEAD
    stacked = projected.reshape(doc_count, seq_len, 3, local_heads, HEAD)
    queries = stacked[:, :, 0]
    key_heads = stacked[:, :, 1]
    values = stacked[:, :, 2]
    scores = jnp.einsum(
        "bqhe,bkhe->bhqk", queries, key_heads, preferred_element_type=jnp.float32
    ) * HEAD ** (-0.5)
    positions = jnp.arange(seq_len, dtype=jnp.int32)
    key_valid = positions[None, :] < doc_lengths[:, None]
    scores = jnp.where(key_valid[:, None, None, :], scores, -jnp.inf)
    attention = jax.nn.softmax(scores, axis=-1).astype(jnp.bfloat16)
    context = jnp.einsum(
        "bhqk,bkhe->bqhe", attention, values, preferred_element_type=jnp.float32
    ).astype(jnp.bfloat16)
    context = context.reshape(doc_count, seq_len, local_heads * HEAD)
    attn_part = jnp.einsum("bsf,fd->bsd", context, out_full, preferred_element_type=jnp.float32)
    residual = residual + lax.psum(attn_part.astype(jnp.bfloat16), "mp").astype(jnp.float32)
    hidden_normed = normalize(residual).astype(jnp.bfloat16)
    activated = jax.nn.gelu(
        jnp.einsum("bsd,df->bsf", hidden_normed, up_full, preferred_element_type=jnp.float32),
        approximate=False,
    ).astype(jnp.bfloat16)
    mlp_part = jnp.einsum("bsf,fd->bsd", activated, down_full, preferred_element_type=jnp.float32)
    valid = key_valid.astype(jnp.float32)
    pooled_part = jnp.sum(valid[:, :, None] * mlp_part, axis=1)
    pooled = lax.psum_scatter(pooled_part, "mp", scatter_dimension=0, tiled=True)
    new_count = pooled.shape[0]
    my_valid = lax.dynamic_slice_in_dim(valid, mp_index * new_count, new_count, 0)
    my_residual = lax.dynamic_slice_in_dim(residual, mp_index * new_count, new_count, 0)
    my_lengths = lax.dynamic_slice_in_dim(doc_lengths, mp_index * new_count, new_count, 0)
    pooled = (pooled + jnp.sum(my_valid[:, :, None] * my_residual, axis=1)) / my_lengths[
        :, None
    ].astype(jnp.float32)
    row_units = jnp.concatenate(
        [unit_rows(pooled), unit_rows(stored_embed.astype(jnp.float32))], axis=0
    )
    row_count = row_units.shape[0]
    clusters = CL_OWN * lax.axis_size("dp")
    capacity = (row_count + clusters - 1) // clusters + (row_count + 2 * clusters - 1) // (
        2 * clusters
    )
    labels_flat = doc_labels[:, 0]
    member = (labels_flat[:, None] == jnp.arange(clusters, dtype=jnp.int32)[None, :]).astype(
        jnp.int32
    )
    before = jnp.cumsum(member, axis=0) - member
    slot_index = jnp.sum(before * member, axis=1)
    target = labels_flat * capacity + slot_index
    placed = target[None, :] == jnp.arange(clusters * capacity, dtype=jnp.int32)[:, None]
    send_units = jnp.dot(
        placed.astype(jnp.bfloat16), row_units, preferred_element_type=jnp.float32
    ).astype(jnp.bfloat16)
    send_units = send_units.reshape(clusters, capacity, row_units.shape[1])
    send_order = (jnp.sum(jnp.where(placed, doc_order[None, :] + 1, 0), axis=1) - 1).reshape(
        clusters, capacity
    )
    owned_units, owned_order = (
        lax.all_to_all(send_units, "dp", split_axis=0, concat_axis=1, tiled=True),
        lax.all_to_all(send_order, "dp", split_axis=0, concat_axis=1, tiled=True),
    )
    block_units, block_order = (
        lax.all_gather(owned_units, ("mp", "rep"), axis=1, tiled=True),
        lax.all_gather(owned_order, ("mp", "rep"), axis=1, tiled=True),
    )
    similar = jnp.einsum(
        "cqd,ckd->cqk", owned_units, block_units, preferred_element_type=jnp.float32
    )
    earlier = (block_order[:, None, :] >= 0) & (block_order[:, None, :] < owned_order[:, :, None])
    largest = jnp.max(jnp.where(earlier, similar, -2.0), axis=2)
    best_slot = jnp.where(largest < -1.5, 0.0, largest)
    returned = lax.all_to_all(best_slot, "dp", split_axis=1, concat_axis=0, tiled=True)
    return jnp.sum(jnp.where(placed, returned.reshape(-1)[:, None], 0.0), axis=0)


def solution(mesh):
    placed = (
        P(("parts", "dp", "rep"), None, None),
        P(("parts", "dp", "rep")),
        P("dp", None, "mp"),
        P("mp", "dp"),
        P("dp", "mp"),
        P("mp", "dp"),
        P(("parts", "dp", "mp", "rep"), None),
        P(("parts", "dp", "mp", "rep"), None),
        P(("parts", "dp", "mp", "rep")),
    )
    return jax.shard_map(
        shards,
        mesh=mesh,
        in_specs=placed,
        out_specs=P(("parts", "dp", "mp", "rep")),
        check_vma=False,
    )
```

profile of v0, /device:TPU:0, one launch (start us, length us, event | category | flops | bytes accessed | tf_op | source)
XLA Modules:
  0.0 341.1 jit_solution(6374969925207892974)
XLA Ops:
  6.6 1.9 constant_dynamic-slice_fusion.4
  8.5 0.0 all-gather.10.cloned.1.call-start
  8.5 40.2 %all-gather.8.cloned.1.call-done = bf16[1024,3,256]{2,0,1:T(8,128)(2,1)} async-done(((bf16[256,3,256]{2,0,1:T(8,128)(2,1)}), bf16[1024,3,256]{2,0,1:T(8,128)(2,1)}) %all-gather.8.cloned.1.call-update) | async-done | bytes 1572880 | tf_op jit(solution)/shard_map/all_gather | solution.py:31
  48.8 0.0 all-gather.12.cloned.1.call-start
  48.8 0.9 constant_dynamic-slice_fusion.3
  49.8 16.4 %all_gather.33 = bf16[256,1024]{1,0:T(8,128)(2,1)} all-gather(bf16[256,256]{1,0:T(8,128)(2,1)S(1)} %constant_dynamic-slice_fusion.3), channel_id=1, replica_groups=mesh['parts'=2,'dp'=4,'mp'=2,'rep'=2] {'dp'}, dimensions={1}, use_global_device_ids=true | all-gather | bytes 655360 | tf_op jit(solution)/shard_map/all_gather | solution.py:32
  66.2 0.0 all-gather.14.cloned.1.call-start
  66.3 0.9 constant_dynamic-slice_fusion.2
  67.2 0.0 all-gather.18.cloned.1.call-start
  67.2 1.9 constant_dynamic-slice_fusion.1
  69.1 0.0 all-reduce.4.cloned.1.call-start
  69.2 0.3 convert_reduce_fusion
  69.5 0.7 fusion.13
  70.2 0.1 fusion.119
  70.3 7.1 %fusion.55 = bf16[4,256,3,512]{3,1,2,0:T(8,128)(2,1)} fusion(bf16[1024,3,512]{2,0,1:T(8,128)(2,1)} %all-gather.10.cloned.1.call-done, bf16[4,256,1024]{2,1,0:T(8,128)(2,1)S(1)} %copy-done.2, f32[4,256]{1,0:T(4,128)S(1)} %add_rsqrt_fusion.1, f32[4,256]{1,0:T(4,128)S(1)} %broadcast_multiply_fusion.1), kind=kOutput, calls=%fused_computation.76 | convolution fusion | flops 3226992640 | bytes 8396800 | tf_op jit(solution)/shard_map/bsd,dte->bste/dot_general | solution.py:46
  77.5 4.7 %copy.40 = bf16[4,256,3,512]{1,3,0,2:T(8,128)(2,1)} copy(bf16[4,256,3,512]{3,1,2,0:T(8,128)(2,1)} %fusion.55) | data formatting | bytes 6291456 | tf_op jit(solution)/shard_map/reshape | solution.py:50
  82.1 2.9 fusion.74
  85.1 2.9 fusion.122
  88.0 3.1 fusion.66
  91.1 4.3 %convolution_convert_fusion = bf16[4,256,1024]{2,1,0:T(8,128)(2,1)} fusion(bf16[4,256,512]{1,2,0:T(8,128)(2,1)} %bitcast.56, bf16[512,1024]{1,0:T(8,128)(2,1)} %all-gather.12.cloned.1.call-done), kind=kOutput, calls=%fused_computation.85 | convolution fusion | flops 1074790400 | bytes 4194304 | tf_op jit(solution)/shard_map/bsf,fd->bsd/dot_general | solution.py:65
  95.5 0.0 all-gather.16.cloned.1.call-start
  95.5 26.9 %all-gather.14.cloned.1.call-done = bf16[1024,1024]{1,0:T(8,128)(2,1)} async-done(((bf16[256,1024]{1,0:T(8,128)(2,1)}), bf16[1024,1024]{1,0:T(8,128)(2,1)}) %all-gather.14.cloned.1.call-update) | async-done | bytes 2097168 | tf_op jit(solution)/shard_map/all_gather | solution.py:33
  122.5 0.0 all-gather.20.cloned.1.call-start
  122.5 46.4 %all-gather.18.cloned.1.call-done = bf16[1024,1024]{1,0:T(8,128)(2,1)} async-done(((bf16[1024,256]{1,0:T(8,128)(2,1)}), bf16[1024,1024]{1,0:T(8,128)(2,1)}) %all-gather.18.cloned.1.call-update) | async-done | bytes 2097168 | tf_op jit(solution)/shard_map/all_gather | solution.py:34
  168.9 0.1 fusion.82
  169.0 0.1 reduce_window_sum.11
  169.1 0.2 select_reduce_fusion.2
  169.3 0.1 select_reduce_fusion.1
  169.4 0.7 sub.35
  170.1 3.4 %all-to-all-start = ((s32[4,1,26]{2,1,0:T(1,128)}), s32[4,1,26]{2,1,0:T(1,128)S(1)}, u32[]{:S(2)}, u32[]{:S(2)}) async-start(s32[4,1,26]{2,1,0:T(1,128)} %bitcast.1), calls=%async_computation | async-start | bytes 4096 | tf_op jit(solution)/shard_map/all_to_all | solution.py:108
  173.5 0.6 dynamic-slice.1
  174.8 0.1 dynamic-slice_convert_fusion
  174.9 0.1 fusion.77
  175.0 0.1 fusion.78
  175.1 57.1 %all-reduce.4.cloned.1.call-done = bf16[4,256,1024]{2,1,0:T(8,128)(2,1)} async-done(((bf16[4,256,1024]{2,1,0:T(8,128)(2,1)}), bf16[4,256,1024]{2,1,0:T(8,128)(2,1)}) %all-reduce.4.cloned.1.call-update) | async-done | bytes 2097168 | tf_op jit(solution)/shard_map/psum | solution.py:66
  232.2 2.2 fusion.120
  234.4 4.4 %multiply_reduce_fusion.1 = (f32[4,256]{1,0:T(4,128)S(1)}, f32[4,256,1024]{2,1,0:T(8,128)}) fusion(f32[4,256]{1,0:T(4,128)S(1)} %broadcast_multiply_fusion, bf16[4,256,1024]{2,1,0:T(8,128)(2,1)} %all-reduce.4.cloned.1.call-done, bf16[4,256,1024]{2,1,0:T(8,128)(2,1)S(1)} %copy-done.2), kind=kLoop, calls=%fused_computation.69 | loop fusion | flops 6290432 | bytes 8396800 | tf_op jit(solution)/shard_map/reduce_sum | solution.py:12
  238.9 8.7 %all-gather.16.cloned.1.call-done = bf16[1024,2048]{1,0:T(8,128)(2,1)} async-done(((bf16[1024,1024]{1,0:T(8,128)(2,1)}), bf16[1024,2048]{1,0:T(8,128)(2,1)}) %all-gather.16.cloned.1.call-update) | async-done | bytes 4194320 | tf_op jit(solution)/shard_map/all_gather | solution.py:39
  247.6 12.9 %fusion.65 = (u8[256,2048]{1,0:T(8,128)(4,1)}, u8[256,2048]{1,0:T(8,128)(4,1)}, f32[4,256,2048]{2,1,0:T(8,128)}) fusion(bf16[1024,2048]{1,0:T(8,128)(2,1)} %all-gather.16.cloned.1.call-done, f32[4,256]{1,0:T(4,128)S(1)} %add_rsqrt_fusion, f32[4,256]{1,0:T(4,128)S(1)} %broadcast_multiply_fusion, bf16[4,256,1024]{2,1,0:T(8,128)(2,1)} %all-reduce.4.cloned.1.call-done, ...), kind=kOutput, calls=%fused_computation.84 | convolution fusion | flops 4327473152 | bytes 17833984 | tf_op jit(solution)/shard_map/bsd,df->bsf/dot_general | solution.py:69
  260.4 3.6 %all-gather.20.cloned.1.call-done = bf16[2048,1024]{1,0:T(8,128)(2,1)} async-done(((bf16[1024,1024]{1,0:T(8,128)(2,1)}), bf16[2048,1024]{1,0:T(8,128)(2,1)}) %all-gather.20.cloned.1.call-update) | async-done | bytes 4194320 | tf_op jit(solution)/shard_map/all_gather | solution.py:40
  264.0 25.3 %multiply_reduce_fusion = f32[4,1024]{1,0:T(4,128)S(1)} fusion(f32[4,256]{1,0:T(4,128)S(1)} %get-tuple-element.11, bf16[2048,1024]{1,0:T(8,128)(2,1)} %all-gather.20.cloned.1.call-done, f32[4,256,2048]{2,1,0:T(8,128)} %get-tuple-element.15, u8[256,2048]{1,0:T(8,128)(4,1)} %get-tuple-element.6, u8[256,2048]{1,0:T(8,128)(4,1)} %get-tuple-element.5), kind=kOutput, calls=%fused_computation.38 | convolution fusion | flops 4443860992 | bytes 13651968 | tf_op jit(solution)/shard_map/bsf,fd->bsd/dot_general | solution.py:72
  289.4 8.4 %all-reduce.1 = f32[4,1024]{1,0:T(4,128)S(1)} all-reduce(f32[4,1024]{1,0:T(4,128)S(1)} %multiply_reduce_fusion), channel_id=2, replica_groups=mesh['parts'=2,'dp'=4,'mp'=2,'rep'=2] {'mp'}, use_global_device_ids=true, to_apply=%region_11.12.clone | all-reduce | flops 4096 | bytes 32768
  297.7 1.8 multiply_reduce_fusion.2
  299.6 0.2 multiply_reduce_fusion.3
  299.8 0.1 multiply_convert_fusion.2
  299.8 0.3 convolution_convert_fusion.1
  300.2 0.8 reshape.183
  300.9 4.6 %all-to-all-start.1 = ((bf16[4,26,1024]{2,1,0:T(8,128)(2,1)}), bf16[4,26,1024]{2,1,0:T(8,128)(2,1)S(1)}, u32[]{:S(2)}, u32[]{:S(2)}) async-start(bf16[4,26,1024]{2,1,0:T(8,128)(2,1)} %reshape.183), calls=%async_computation.1 | async-start | bytes 524288 | tf_op jit(solution)/shard_map/all_to_all | solution.py:107
  305.5 0.6 dynamic-slice
  306.8 0.5 broadcast.183
  307.3 0.7 reduce.12
  308.0 0.1 reshape.186
  308.0 0.2 dynamic-update-slice
  308.2 4.3 %all-reduce = s32[416]{0:T(512)S(1)} all-reduce(s32[416]{0:T(512)S(1)} %dynamic-update-slice), channel_id=1, replica_groups=mesh['parts'=2,'dp'=4,'mp'=2,'rep'=2] {'mp','rep'}, use_global_device_ids=true, to_apply=%add | all-reduce | flops 416 | bytes 3328 | tf_op jit(solution)/shard_map/broadcast_in_dim | solution.py:117
  312.5 0.1 all_to_all.30
  312.6 8.6 %all_gather.39 = bf16[1,416,1024]{2,1,0:T(8,128)(2,1)S(1)} all-gather(bf16[1,104,1024]{2,1,0:T(8,128)(2,1)S(1)} %all_to_all.30), channel_id=1, replica_groups=mesh['parts'=2,'dp'=4,'mp'=2,'rep'=2] {'mp','rep'}, dimensions={1}, use_global_device_ids=true | all-gather | bytes 1064960 | tf_op jit(solution)/shard_map/all_gather | solution.py:111
  321.2 0.1 reshape.184
  321.3 0.5 fusion.71
  321.8 0.1 reduce_max.22
  321.9 10.4 %all_to_all.35 = f32[1,4,26]{2,0,1:T(1,128)S(1)} all-to-all(f32[1,4,26]{2,0,1:T(1,128)S(1)} %bitcast.53), channel_id=1, replica_groups=mesh['parts'=2,'dp'=4,'mp'=2,'rep'=2] {'dp'}, dimensions={1} | all-to-all | bytes 832 | tf_op jit(solution)/shard_map/all_to_all | solution.py:120
  332.3 0.5 broadcast.184
  332.8 0.7 reduce.13
  333.5 0.1 broadcast_in_dim.76
  333.6 0.7 select_reduce_fusion
  (43 shorter events, 0.3 us)
Async XLA Ops:
  6.5 59.7 %copy-start = (bf16[256,2048]{1,0:T(8,128)(2,1)S(1)}, bf16[256,2048]{1,0:T(8,128)(2,1)}, u32[]{:S(2)}) copy-start(bf16[256,2048]{1,0:T(8,128)(2,1)} %param.13) | copy-start | bytes 3145732
  6.5 62.6 %copy-start.2 = (bf16[4,256,1024]{2,1,0:T(8,128)(2,1)S(1)}, bf16[4,256,1024]{2,1,0:T(8,128)(2,1)}, u32[]{:S(2)}) copy-start(bf16[4,256,1024]{2,1,0:T(8,128)(2,1)} %param.9) | copy-start | bytes 6291460
  6.5 63.7 %copy-start.6 = (s32[4]{0:T(128)S(1)}, s32[4]{0:T(128)}, u32[]{:S(2)}) copy-start(s32[4]{0:T(128)} %param.10) | copy-start | bytes 52
  6.5 42.2 %all-gather.8.cloned.1.call-start = ((), (), s32[]{:S(2)}) async-start(), calls=%async_computation.3 | async-start | bytes 1966080 | tf_op jit(solution)/shard_map/all_gather | solution.py:31
  8.5 61.8 %all-gather.10.cloned.1.call-start = ((), (), s32[]{:S(2)}) async-start(), calls=%async_computation.4 | async-start | bytes 4718592 | tf_op jit(solution)/shard_map/all_gather | solution.py:37
  48.8 42.4 %all-gather.12.cloned.1.call-start = ((), (), s32[]{:S(2)}) async-start(), calls=%async_computation.5 | async-start | bytes 1572864 | tf_op jit(solution)/shard_map/all_gather | solution.py:38
  66.2 56.2 %all-gather.14.cloned.1.call-start = ((), (), s32[]{:S(2)}) async-start(), calls=%async_computation.7 | async-start | bytes 2621440 | tf_op jit(solution)/shard_map/all_gather | solution.py:33
  67.2 101.7 %all-gather.18.cloned.1.call-start = ((), (), s32[]{:S(2)}) async-start(), calls=%async_computation.9 | async-start | bytes 2621440 | tf_op jit(solution)/shard_map/all_gather | solution.py:34
  69.1 163.1 %all-reduce.4.cloned.1.call-start = ((), (), s32[]{:S(2)}) async-start(), calls=%async_computation.6 | async-start | bytes 4194304 | tf_op jit(solution)/shard_map/psum | solution.py:66
  91.1 77.8 %copy-start.4 = (s32[65,1]{0,1:T(1,128)S(1)}, s32[65,1]{0,1:T(1,128)}, u32[]{:S(2)}) copy-start(s32[65,1]{0,1:T(1,128)} %param.16) | copy-start | bytes 784
  91.1 78.2 %copy-start.5 = (s32[65]{0:T(128)S(1)}, s32[65]{0:T(128)}, u32[]{:S(2)}) copy-start(s32[65]{0:T(128)} %param.17) | copy-start | bytes 784
  91.1 82.4 %copy-start.8 = (u32[32]{0:T(128)S(1)}, u32[32]{0:T(128)}, u32[]{:S(2)}) copy-start(u32[32]{0:T(128)} %constant.126) | copy-start | bytes 388
  91.1 83.8 %copy-start.3 = (bf16[63,1024]{1,0:T(8,128)(2,1)S(1)}, bf16[63,1024]{1,0:T(8,128)(2,1)}, u32[]{:S(2)}) copy-start(bf16[63,1024]{1,0:T(8,128)(2,1)} %param.15) | copy-start | bytes 387076
  95.5 152.1 %all-gather.16.cloned.1.call-start = ((), (), s32[]{:S(2)}) async-start(), calls=%async_computation.8 | async-start | bytes 6291456 | tf_op jit(solution)/shard_map/all_gather | solution.py:39
  122.5 141.6 %all-gather.20.cloned.1.call-start = ((), (), s32[]{:S(2)}) async-start(), calls=%async_computation.10 | async-start | bytes 6291456 | tf_op jit(solution)/shard_map/all_gather | solution.py:40
  170.1 130.8 %all-to-all-start = ((s32[4,1,26]{2,1,0:T(1,128)}), s32[4,1,26]{2,1,0:T(1,128)S(1)}, u32[]{:S(2)}, u32[]{:S(2)}) async-start(s32[4,1,26]{2,1,0:T(1,128)} %bitcast.1), calls=%async_computation | async-start | bytes 4096 | tf_op jit(solution)/shard_map/all_to_all | solution.py:108
  264.0 41.5 %copy-start.7 = (u32[32]{0:T(128)S(1)}, u32[32]{0:T(128)}, u32[]{:S(2)}) copy-start(u32[32]{0:T(128)} %constant.120) | copy-start | bytes 388
  264.0 70.2 %copy-start.1 = (bf16[256,2048]{1,0:T(8,128)(2,1)S(1)}, bf16[256,2048]{1,0:T(8,128)(2,1)}, u32[]{:S(2)}) copy-start(bf16[256,2048]{1,0:T(8,128)(2,1)} %param.13) | copy-start | bytes 3145732
  300.9 11.6 %all-to-all-start.1 = ((bf16[4,26,1024]{2,1,0:T(8,128)(2,1)}), bf16[4,26,1024]{2,1,0:T(8,128)(2,1)S(1)}, u32[]{:S(2)}, u32[]{:S(2)}) async-start(bf16[4,26,1024]{2,1,0:T(8,128)(2,1)} %reshape.183), calls=%async_computation.1 | async-start | bytes 524288 | tf_op jit(solution)/shard_map/all_to_all | solution.py:107
Sparse Core Ops, SparseCore 0:
  8.9 39.7 all-gather.7
  50.3 10.5 all-gather.9
  66.3 7.5 all-gather.11
  75.4 47.0 all-gather.13
  123.9 44.9 all-gather.17
  171.0 61.1 all-reduce.3
  233.8 13.6 all-gather.15
  249.2 14.8 all-gather.19
where the time goes:
time: 342 us; the launch traced here: 341 us
  waiting for transfers between devices  183 us (54%)
  matrix products  56.5 us (17%)
  blocking collectives  48.1 us (14%)
  other arithmetic  15.5 us (5%)
  between operations  15 us (4%)
  local copies, waits for them, and re-layouts  14.5 us (4%)
  starting transfers between devices  8.31 us (2%)
    psum x1, waiting for transfers between devices, shards(): lax.psum(attn_part.astype(jnp.bfloat16), 'mp').astype(jnp.float32)  57.1 us
    all_gather x1, waiting for transfers between devices, shards(): lax.all_gather(rep_half(w_down, 0), 'dp', axis=1, tiled=True)  46.4 us
    all_gather x1, waiting for transfers between devices, shards(): lax.all_gather(rep_half(w_qkv, 2), 'dp', axis=0, tiled=True)  40.2 us
    all_gather x1, waiting for transfers between devices, shards(): lax.all_gather(rep_half(w_up, 1), 'dp', axis=0, tiled=True)  26.9 us
    dot_general x1, matrix products, shards(): jnp.einsum('bsf,fd->bsd', activated, down_full, preferred_element_type=jn...  25.3 us
    all_gather x1, blocking collectives, shards(): lax.all_gather(rep_half(w_out, 0), 'dp', axis=1, tiled=True)  16.4 us
    dot_general x1, matrix products, shards(): jnp.einsum('bsd,df->bsf', hidden_normed, up_full, preferred_element_type=...  12.9 us
    all_to_all x1, blocking collectives, shards(): lax.all_to_all(best_slot, 'dp', split_axis=1, concat_axis=0, tiled=True)  10.4 us
  transfers between devices with their start and end apart: 10, of which 6 were waited for; matrix products, arithmetic and copies ran while one was open for 24% of the time, Pallas kernels for 0%

commit v1 on v0

v1 whole, which is shorter than its diff:
```python
import functools

import jax
import jax.numpy as jnp
from jax import lax
from jax.experimental import pallas as pl
from jax.experimental.pallas import tpu as pltpu
from jax.sharding import PartitionSpec as P

HEAD = 64
LANES = 128
MESH = pl.DeviceIdType.MESH


def unit_rows(values):
    return (values * lax.rsqrt(jnp.sum(values * values, axis=-1, keepdims=True) + 1e-06)).astype(
        jnp.bfloat16
    )


def normed_rows(values):
    centred = values - jnp.mean(values, axis=-1, keepdims=True)
    spread = jnp.mean(centred * centred, axis=-1, keepdims=True)
    return (centred * lax.rsqrt(spread + 1e-05)).astype(jnp.bfloat16)


def encode_kernel(
    n, mps, splits, len_ref, hid_ref, wq_ref, wo_ref, wu_ref, act_ref, res_ref,
    q_buf, o_buf, u_buf, c_buf, proj, z_send, z_recv, c_send, c_recv, x_send, x_recv, y_send, y_recv,
):
    me, my_mp = lax.axis_index("dp"), lax.axis_index("mp")
    part, rep = lax.axis_index("parts"), lax.axis_index("rep")
    docs, seq, _ = hid_ref.shape
    heads_wide = c_buf.shape[3]
    depth = wq_ref.shape[0]
    out_rows = wo_ref.shape[0]

    def piece(which, source, p, r):
        number = splits[which]
        group = p * 2 + r if number == 4 else p
        if which == 1:
            rows = out_rows // number
            return o_buf.at[my_mp, source, pl.ds(pl.multiple_of(group * rows, 16), rows), :]
        buf = q_buf if which == 0 else u_buf
        wide = buf.shape[1] // number
        return buf.at[
            pl.ds(pl.multiple_of(source * depth, 16), depth),
            pl.ds(pl.multiple_of(group * wide, LANES), wide),
        ]

    def copy_of(which, source, p, r, send, recv, device):
        ref = piece(which, source, p, r)
        return pltpu.make_async_remote_copy(
            src_ref=ref, dst_ref=ref, send_sem=z_send.at[which, source, send],
            recv_sem=z_recv.at[which, source, recv], device_id=device, device_id_type=MESH,
        )

    def right(which, source):
        return copy_of(which, source, part, rep, 0, 0, {"dp": me + 1})

    def left(which, source):
        return copy_of(which, source, part, rep, 4, 0, {"dp": me - 1})

    def across(which, source, p):
        return copy_of(which, source, p, rep, 1, 1, {"parts": 1 - part})

    def beside(which, source, r):
        return copy_of(which, source, part, r, 2, 2, {"rep": 1 - rep})

    def beside_late(which, source, p, r):
        return copy_of(which, source, p, r, 3, 3, {"rep": 1 - rep})

    def own(which):
        @pl.when(me < n - 1)
        def _():
            right(which, me).start()

        @pl.when(me > 0)
        def _():
            left(which, me).start()

    def on_z(which, source, rightward):
        way = right if rightward else left
        way(which, source).wait_recv()

        @pl.when(me < n - 1 if rightward else me > 0)
        def _():
            way(which, source).start()

        across(which, source, part).start()
        if splits[which] == 4:
            beside(which, source, rep).start()

    def on_y(which, source):
        across(which, source, 1 - part).wait_recv()
        if splits[which] == 4:
            beside_late(which, source, 1 - part, rep).start()

    def both(step, fn):
        @pl.when(step <= me)
        def _():
            fn(me - step, True)

        @pl.when(me + step <= n - 1)
        def _():
            fn(me + step, False)

    def steps(which, lo, hi):
        def body(step, carry):
            both(step, lambda source, way: on_z(which, source, way))

            @pl.when(step > 1)
            def _():
                both(step - 1, lambda source, way: on_y(which, source))

            return carry

        lax.fori_loop(lo, hi, body, 0)

    def finish(which):
        both(n - 1, lambda source, way: on_y(which, source))
        if splits[which] == 4:

            def body(step, carry):
                def take(source, way):
                    beside(which, source, 1 - rep).wait_recv()
                    beside_late(which, source, 1 - part, 1 - rep).wait_recv()

                both(step, take)
                return carry

            lax.fori_loop(1, n, body, 0)

    def sent(which):
        @pl.when(me < n - 1)
        def _():
            right(which, me).wait_send()

        @pl.when(me > 0)
        def _():
            left(which, me).wait_send()

        def body(step, carry):
            def drop(source, way):
                @pl.when(me < n - 1 if way else me > 0)
                def _():
                    (right if way else left)(which, source).wait_send()

                across(which, source, part).wait_send()
                if splits[which] == 4:
                    beside(which, source, rep).wait_send()
                    beside_late(which, source, 1 - part, rep).wait_send()

            both(step, drop)
            return carry

        lax.fori_loop(1, n, body, 0)

    def other(k):
        return lax.rem(my_mp + k, mps)

    def context_copy(owner, k, doc):
        ref = c_buf.at[owner, doc]
        return pltpu.make_async_remote_copy(
            src_ref=ref, dst_ref=ref, send_sem=c_send.at[k, doc], recv_sem=c_recv.at[owner, doc],
            device_id={"mp": other(k)}, device_id_type=MESH,
        )

    half = out_rows // 2

    def out_half(owner, r):
        return o_buf.at[owner, :, pl.ds(pl.multiple_of(r * half, 16), half), :]

    def out_copy(owner, k):
        ref = out_half(owner, rep)
        return pltpu.make_async_remote_copy(
            src_ref=ref, dst_ref=ref, send_sem=x_send.at[k], recv_sem=x_recv.at[owner],
            device_id={"mp": other(k)}, device_id_type=MESH,
        )

    def out_beside(owner, r):
        ref = out_half(owner, r)
        return pltpu.make_async_remote_copy(
            src_ref=ref, dst_ref=ref, send_sem=y_send.at[owner], recv_sem=y_recv.at[owner],
            device_id={"rep": 1 - rep}, device_id_type=MESH,
        )

    q_buf[pl.ds(pl.multiple_of(me * depth, 16), depth), :] = wq_ref[...]
    o_buf[my_mp, me] = wo_ref[...]
    u_buf[pl.ds(pl.multiple_of(me * depth, 16), depth), :] = wu_ref[...]

    barrier = pltpu.get_barrier_semaphore()

    @pl.when(me < n - 1)
    def _():
        pl.semaphore_signal(barrier, inc=1, device_id={"dp": me + 1}, device_id_type=MESH)

    @pl.when(me > 0)
    def _():
        pl.semaphore_signal(barrier, inc=1, device_id={"dp": me - 1}, device_id_type=MESH)

    pl.semaphore_signal(barrier, inc=1, device_id={"parts": 1 - part}, device_id_type=MESH)
    pl.semaphore_signal(barrier, inc=1, device_id={"rep": 1 - rep}, device_id_type=MESH)
    for k in range(1, mps):
        pl.semaphore_signal(barrier, inc=1, device_id={"mp": other(k)}, device_id_type=MESH)

    inner = (me > 0) & (me < n - 1)

    @pl.when(inner)
    def _():
        pl.semaphore_wait(barrier, 3 + mps)

    @pl.when(jnp.logical_not(inner))
    def _():
        pl.semaphore_wait(barrier, 2 + mps)

    own(0)
    own(1)
    steps(0, 1, n - 1)
    own(2)
    steps(0, n - 1, n)
    finish(0)

    lanes = lax.broadcasted_iota(jnp.int32, (1, LANES), 1) < HEAD
    keys_at = lax.broadcasted_iota(jnp.int32, (1, seq), 1)
    cuts = [1 + (n - 1) * k // 3 for k in range(4)]

    def attend(doc, carry):
        normed = normed_rows(hid_ref[doc].astype(jnp.float32))
        proj[...] = jnp.dot(normed, q_buf[...], preferred_element_type=jnp.float32).astype(jnp.bfloat16)
        visible = keys_at < len_ref[doc]

        for pair in range(heads_wide // LANES):
            queries = proj[:, pair * LANES:(pair + 1) * LANES]
            keys = proj[:, heads_wide + pair * LANES:heads_wide + (pair + 1) * LANES]
            values = proj[:, 2 * heads_wide + pair * LANES:2 * heads_wide + (pair + 1) * LANES]
            queries = queries * jnp.asarray(HEAD ** (-0.5), jnp.bfloat16)
            blank = jnp.zeros_like(queries)
            made = []
            for mine in (lanes, jnp.logical_not(lanes)):
                scores = lax.dot_general(
                    jnp.where(mine, queries, blank), keys, (((1,), (1,)), ((), ())),
                    preferred_element_type=jnp.float32,
                )
                scores = jnp.where(visible, scores, -jnp.inf)
                weights = jnp.exp(scores - jnp.max(scores, axis=1, keepdims=True))
                total = jnp.sum(weights, axis=1, keepdims=True)
                weights = (weights / total).astype(jnp.bfloat16)
                made.append(jnp.dot(weights, values, preferred_element_type=jnp.float32))
            context = jnp.where(lanes, made[0], made[1]).astype(jnp.bfloat16)
            c_buf[my_mp, doc, :, pair * LANES:(pair + 1) * LANES] = context

        for k in range(1, mps):
            context_copy(my_mp, k, doc).start()

        @pl.when(doc == 0)
        def _():
            steps(1, 1, n)
            finish(1)
            for k in range(1, mps):
                out_copy(my_mp, k).start()

        for k in range(3):
            @pl.when(doc == min(k + 1, docs - 1))
            def _():
                steps(2, cuts[k], cuts[k + 1])

        return carry

    lax.fori_loop(0, docs, attend, 0)
    for k in range(1, mps):
        out_copy(other(k), k).wait_recv()
        out_beside(other(k), rep).start()
    finish(2)
    for k in range(1, mps):
        out_beside(other(k), 1 - rep).wait_recv()

    def feed(doc, carry):
        for k in range(1, mps):
            context_copy(other(k), k, doc).wait_recv()
        residual = hid_ref[doc].astype(jnp.float32)
        for owner in range(mps):
            context = c_buf[owner, doc]
            product = jnp.concatenate(
                [jnp.dot(context, o_buf[owner, j], preferred_element_type=jnp.float32) for j in range(n)], axis=1
            )
            residual = residual + product.astype(jnp.bfloat16).astype(jnp.float32)
        valid = lax.broadcasted_iota(jnp.int32, (seq, 1), 0) < len_ref[doc]
        res_ref[doc] = jnp.sum(jnp.where(valid, residual, 0.0), axis=0, keepdims=True)
        normed = normed_rows(residual)
        wide = u_buf.shape[1]
        block = wide // 4
        for k in range(4):
            hidden = jnp.dot(normed, u_buf[:, k * block:(k + 1) * block], preferred_element_type=jnp.float32)
            hidden = 0.5 * hidden * (1.0 + lax.erf(hidden * (0.5 ** 0.5)))
            hidden = hidden.astype(jnp.bfloat16).astype(jnp.float32)
            act_ref[doc, :, k * block:(k + 1) * block] = jnp.sum(
                jnp.where(valid, hidden, 0.0), axis=0, keepdims=True
            )
        return carry

    lax.fori_loop(0, docs, feed, 0)

    for which in range(3):
        sent(which)

    def unsent(doc, carry):
        for k in range(1, mps):
            context_copy(my_mp, k, doc).wait_send()
        return carry

    lax.fori_loop(0, docs, unsent, 0)
    for k in range(1, mps):
        out_copy(my_mp, k).wait_send()
        out_beside(other(k), rep).wait_send()


def encode(lengths, hidden, w_qkv, w_out, w_up):
    n, mps = lax.axis_size("dp"), lax.axis_size("mp")
    docs, seq, width = hidden.shape
    splits = tuple(
        4 if extent % (4 * unit) == 0 else 2
        for extent, unit in ((w_qkv.shape[1], LANES), (w_out.shape[0], 16), (w_up.shape[1], LANES))
    )
    heads_wide = w_qkv.shape[1] // 3
    whole = pl.BlockSpec(memory_space=pltpu.VMEM)
    dma = pltpu.SemaphoreType.DMA
    return pl.pallas_call(
        functools.partial(encode_kernel, n, mps, splits),
        out_shape=(
            jax.ShapeDtypeStruct((docs, 1, w_up.shape[1]), jnp.float32),
            jax.ShapeDtypeStruct((docs, 1, width), jnp.float32),
        ),
        in_specs=[pl.BlockSpec(memory_space=pltpu.SMEM)] + [whole] * 4,
        out_specs=(whole, whole),
        scratch_shapes=[
            pltpu.VMEM((width, w_qkv.shape[1]), jnp.bfloat16),
            pltpu.VMEM((mps, n) + w_out.shape, jnp.bfloat16),
            pltpu.VMEM((width, w_up.shape[1]), jnp.bfloat16),
            pltpu.VMEM((mps, docs, seq, heads_wide), jnp.bfloat16),
            pltpu.VMEM((seq, w_qkv.shape[1]), jnp.bfloat16),
            dma((3, n, 5)),
            dma((3, n, 4)),
            dma((mps, docs)),
            dma((mps, docs)),
            dma((mps,)),
            dma((mps,)),
            dma((mps,)),
            dma((mps,)),
        ],
        compiler_params=pltpu.CompilerParams(
            collective_id=0, has_side_effects=True, vmem_limit_bytes=52 * 1024 * 1024
        ),
        cost_estimate=pl.CostEstimate(flops=12 * 10**9, bytes_accessed=10**8, transcendentals=10**6),
    )(lengths, hidden, w_qkv, w_out, w_up)


def pool_kernel(n, mps, reps, act_ref, res_ref, w_ref, out_ref, a_buf, r_buf, a_send, a_recv, r_send, r_recv, p_send, p_recv):
    me, my_mp, rep = lax.axis_index("dp"), lax.axis_index("mp"), lax.axis_index("rep")
    count = n * mps * reps
    place = (me * mps + my_mp) * reps + rep

    def at(number):
        return {"dp": number // (mps * reps), "mp": number // reps % mps, "rep": number % reps}

    barrier = pltpu.get_barrier_semaphore()

    def greet(k, carry):
        pl.semaphore_signal(barrier, inc=1, device_id=at(lax.rem(place + k, count)), device_id_type=MESH)
        return carry

    lax.fori_loop(1, count, greet, 0)
    pl.semaphore_wait(barrier, count - 1)

    def act_copy(source, target):
        return pltpu.make_async_remote_copy(
            src_ref=act_ref, dst_ref=a_buf.at[source], send_sem=a_send.at[target], recv_sem=a_recv.at[source],
            device_id={"dp": target}, device_id_type=MESH,
        )

    def res_copy(source, target):
        return pltpu.make_async_remote_copy(
            src_ref=res_ref.at[target], dst_ref=r_buf.at[source], send_sem=r_send.at[target],
            recv_sem=r_recv.at[source], device_id={"dp": target}, device_id_type=MESH,
        )

    def give(k, carry):
        target = lax.rem(me + k, n)
        act_copy(me, target).start()
        res_copy(me, target).start()
        return carry

    lax.fori_loop(1, n, give, 0)
    a_buf[me] = act_ref[...]
    r_buf[me] = res_ref[me]

    def take(k, carry):
        source = lax.rem(me + k, n)
        act_copy(source, source).wait()
        res_copy(source, source).wait()
        return carry

    lax.fori_loop(1, n, take, 0)
    acts = jnp.concatenate([a_buf[j] for j in range(n)], axis=0)
    high = acts.astype(jnp.bfloat16)
    low = (acts - high.astype(jnp.float32)).astype(jnp.bfloat16)
    part = jnp.dot(high, w_ref[...], preferred_element_type=jnp.float32)
    part = part + jnp.dot(low, w_ref[...], preferred_element_type=jnp.float32)
    rest = jnp.concatenate([r_buf[j] for j in range(n)], axis=0)
    out_ref[place] = part + jnp.where(my_mp == 0, 1.0, 0.0) * rest

    def part_copy(source, target):
        return pltpu.make_async_remote_copy(
            src_ref=out_ref.at[source], dst_ref=out_ref.at[source], send_sem=p_send.at[target],
            recv_sem=p_recv.at[source], device_id=at(target), device_id_type=MESH,
        )

    def share(k, carry):
        part_copy(place, lax.rem(place + k, count)).start()
        return carry

    lax.fori_loop(1, count, share, 0)

    def collect(k, carry):
        source = lax.rem(place + k, count)
        part_copy(source, source).wait()
        return carry

    lax.fori_loop(1, count, collect, 0)


def pool(acts, rest, w_down):
    n, mps, reps = lax.axis_size("dp"), lax.axis_size("mp"), lax.axis_size("rep")
    docs = acts.shape[0]
    count = n * mps * reps
    whole = pl.BlockSpec(memory_space=pltpu.VMEM)
    dma = pltpu.SemaphoreType.DMA
    return pl.pallas_call(
        functools.partial(pool_kernel, n, mps, reps),
        out_shape=jax.ShapeDtypeStruct((count, n * docs, w_down.shape[1]), jnp.float32),
        in_specs=[whole] * 3,
        out_specs=whole,
        scratch_shapes=[
            pltpu.VMEM((n,) + acts.shape, jnp.float32),
            pltpu.VMEM(rest.shape, jnp.float32),
            dma((n,)), dma((n,)), dma((n,)), dma((n,)), dma((count,)), dma((count,)),
        ],
        compiler_params=pltpu.CompilerParams(
            collective_id=1, has_side_effects=True, vmem_limit_bytes=52 * 1024 * 1024
        ),
    )(acts, rest, w_down)


def shards(hidden_in, doc_lengths, w_qkv, w_out, w_up, w_down, stored_embed, doc_labels, doc_order):
    n, mps, reps = lax.axis_size("dp"), lax.axis_size("mp"), lax.axis_size("rep")
    docs, _, width = hidden_in.shape
    place = (lax.axis_index("dp") * mps + lax.axis_index("mp")) * reps + lax.axis_index("rep")
    blocks = n * mps * reps
    rows = doc_order.shape[0]
    new_count = docs // mps
    ranks = blocks * rows

    stored_units = unit_rows(stored_embed.astype(jnp.float32))
    labels = doc_labels[:, 0]
    own_key = labels * ranks + doc_order
    spare = -stored_units.shape[0] % 16
    all_stored = lax.all_gather(
        jnp.pad(stored_units, ((0, spare), (0, 0))), ("dp", "mp", "rep"), axis=0, tiled=True
    )
    keys = lax.all_gather(own_key, ("dp", "mp", "rep"), axis=0, tiled=False)
    stored_keys = jnp.pad(keys[:, new_count:], ((0, 0), (0, spare)), constant_values=-1)

    acts, rest = encode(doc_lengths, hidden_in, w_qkv.reshape(w_qkv.shape[0], -1), w_out, w_up)
    scale = 1.0 / doc_lengths[:, None].astype(jnp.float32)
    acts = acts[:, 0] * scale
    rest = (rest[:, 0] * scale).reshape(docs, n, width // n).transpose(1, 0, 2)
    parts = pool(acts, rest, w_down)
    pooled = jnp.sum(parts.reshape(n, mps, reps, n, docs, width // n), axis=1)
    pooled = pooled.transpose(2, 1, 3, 0, 4).reshape(n, reps, mps, new_count, width)
    new_units = unit_rows(pooled).transpose(0, 2, 1, 3, 4).reshape(blocks * new_count, width)
    own_new = lax.dynamic_slice_in_dim(new_units, place * new_count, new_count, 0)
    own_rows = jnp.concatenate([own_new, stored_units], axis=0)

    def best_of(units, unit_keys):
        similar = lax.dot_general(
            own_rows, units, (((1,), (1,)), ((), ())), preferred_element_type=jnp.float32
        )
        unit_keys = unit_keys.reshape(1, -1)
        earlier = (unit_keys < own_key[:, None]) & (unit_keys >= (labels * ranks)[:, None])
        return jnp.max(jnp.where(earlier, similar, -2.0), axis=1)

    largest = jnp.maximum(best_of(all_stored, stored_keys), best_of(new_units, keys[:, :new_count]))
    return jnp.where(largest < -1.5, 0.0, largest)


def solution(mesh):
    placed = (
        P(("parts", "dp", "rep"), None, None),
        P(("parts", "dp", "rep")),
        P("dp", None, "mp"),
        P("mp", "dp"),
        P("dp", "mp"),
        P("mp", "dp"),
        P(("parts", "dp", "mp", "rep"), None),
        P(("parts", "dp", "mp", "rep"), None),
        P(("parts", "dp", "mp", "rep")),
    )
    return jax.shard_map(
        shards,
        mesh=mesh,
        in_specs=placed,
        out_specs=P(("parts", "dp", "mp", "rep")),
        check_vma=False,
    )
```

time: 342 us -> 131 us (0.38)
  waiting for transfers between devices: 183 us -> 0.04 us
  Pallas kernels: 0 us -> 93.4 us
  matrix products: 56.5 us -> 2.66 us
  blocking collectives: 48.1 us -> 13.5 us
  other arithmetic: 15.5 us -> 3.24 us
  local copies, waits for them, and re-layouts: 14.5 us -> 3.86 us
  starting transfers between devices: 8.31 us -> 0.01 us
    all_gather x7 -> x1, waiting for transfers between devices: 126 us -> 0.02 us  [shards(): lax.all_gather(jnp.pad(stored_units, ((0, spare), (0, 0))), ('dp', 'mp',...]
    pallas_call x0 -> x2, Pallas kernels: none -> 93.4 us  [the longest x1 79.4 us: encode(): pl.pallas_call(functools.partial(encode_kernel, n, mps, splits), out_shap...]
    psum x1 -> x0, waiting for transfers between devices: 57.1 us -> none  [shards(): lax.psum(attn_part.astype(jnp.bfloat16), 'mp').astype(jnp.float32)]
    dot_general x8 -> x2, matrix products: 56.5 us -> 2.66 us  [best_of(): lax.dot_general(own_rows, units, (((1,), (1,)), ((), ())), preferred_elem...]
    all_gather x2 -> x0, blocking collectives: 25.1 us -> none  [the longest x1 16.4 us: shards(): lax.all_gather(rep_half(w_out, 0), 'dp', axis=1, tiled=True)]
    all_to_all x1 -> x0, blocking collectives: 10.4 us -> none  [shards(): lax.all_to_all(best_slot, 'dp', split_axis=1, concat_axis=0, tiled=True)]
    reduce_sum x8 -> x1, other arithmetic: 10.4 us -> 0.07 us  [shards(): pooled = jnp.sum(parts.reshape(n, mps, reps, n, docs, width // n), axis=1)]
    all_to_all x2 -> x0, starting transfers between devices: 8.03 us -> none  [the longest x1 4.61 us: shards(): lax.all_to_all(send_units, 'dp', split_axis=0, concat_axis=1, tiled=True)]
  transfers between devices with their start and end apart: 10 -> 1, of which waited for: 6 -> 0; matrix products, arithmetic and copies ran while one was open for 24% -> 3% of each run, Pallas kernels for 0% -> 71%
where the time goes in v1:
time: 131 us
  Pallas kernels  93.4 us (71%)
  between operations  14.3 us (11%)
  blocking collectives  13.5 us (10%)
  local copies, waits for them, and re-layouts  3.86 us (3%)
  other arithmetic  3.24 us (2%)
  matrix products  2.66 us (2%)
    pallas_call x1, Pallas kernels, encode(): pl.pallas_call(functools.partial(encode_kernel, n, mps, splits), out_shap...  79.4 us
    pallas_call x1, Pallas kernels, pool(): pl.pallas_call(functools.partial(pool_kernel, n, mps, reps), out_shape=ja...  14 us
    unnamed x1, blocking collectives  13.5 us
    dot_general x2, matrix products, best_of(): lax.dot_general(own_rows, units, (((1,), (1,)), ((), ())), preferred_elem...  2.66 us
  transfers between devices with their start and end apart: 1, of which 0 were waited for; matrix products, arithmetic and copies ran while one was open for 3% of the time, Pallas kernels for 71%

profile of v1, /device:TPU:0, one launch (start us, length us, event | category | flops | bytes accessed | tf_op | source)
XLA Modules:
  0.0 131.0 jit_solution(9652322782150375250)
XLA Ops:
  6.5 0.0 copy-start.2
  6.5 0.0 copy-start.1
  6.5 0.0 all-gather.3.cloned.1.call-start
  6.5 1.1 fusion.2
  7.6 1.0 fusion.3
  8.6 0.7 pad.9
  9.3 0.0 all-gather.3.cloned.1.call-update
  9.3 1.4 %copy.29 = bf16[256,3,512]{0,2,1:T(8,128)(2,1)S(1)} copy(bf16[256,3,512]{2,0,1:T(8,128)(2,1)} %param.11) | data formatting | bytes 1572864 | tf_op args[2]
  10.8 0.3 copy.30.wq_ref
  11.0 0.0 copy-done.2
  11.0 0.0 copy-done.1
  11.1 0.0 copy-start
  11.1 79.4 %shard_map.91 = (f32[4,1,2048]{2,1,0:T(1,128)S(1)}, f32[4,1,1024]{2,1,0:T(1,128)S(1)}) custom-call(s32[4]{0:T(128)S(1)} %copy-done.2, bf16[4,256,1024]{2,1,0:T(8,128)(2,1)} %hid_ref.1, bf16[256,1536]{1,0:T(8,128)(2,1)S(1)} %copy.30.wq_ref, bf16[512,256]{1,0:T(8,128)(2,1)S(1)} %copy-done.1, bf16[256,2048]{1,0:T(8,128)(2,1)} %wu_ref.1), custom_call_target="tpu_custom_call" | custom-call | flops 12000000000 | bytes 100000000 | tf_op jit(solution)/shard_map/pallas_call | solution.py:328
  90.5 0.0 copy-start.5
  90.5 0.0 copy-start.3
  90.5 0.0 copy-start.4
  90.6 0.1 multiply_bitcast_fusion.res_ref
  90.7 0.1 bitcast_multiply_fusion.act_ref
  90.7 0.0 copy-done
  90.8 14.0 %shard_map.92 = f32[16,16,256]{2,1,0:T(8,128)S(1)} custom-call(f32[4,2048]{1,0:T(4,128)S(1)} %bitcast_multiply_fusion.act_ref, f32[4,4,256]{2,1,0:T(4,128)S(1)} %multiply_bitcast_fusion.res_ref, bf16[2048,256]{1,0:T(8,128)(2,1)S(1)} %copy-done), custom_call_target="tpu_custom_call" | custom-call | tf_op jit(solution)/shard_map/pallas_call | solution.py:438
  104.7 0.1 reshape.48
  104.8 0.1 reduce_sum.27
  104.9 0.1 copy.32
  105.0 0.1 reshape.49
  105.1 0.1 multiply_reduce_fusion
  105.2 0.1 copy.35
  105.3 0.1 copy.36
  105.5 0.1 fusion.4
  105.7 0.0 copy-done.5
  105.7 0.6 dynamic-slice
  106.9 0.0 copy-done.3
  106.9 0.0 copy-done.4
  107.0 0.1 fusion.8
  107.1 13.5 %all-reduce.2 = s32[1040]{0:T(1024)S(1)} all-reduce(s32[1040]{0:T(1024)S(1)} %get-tuple-element.9), channel_id=2, replica_groups=mesh['parts'=2,'dp'=4,'mp'=2,'rep'=2] {'dp','mp','rep'}, use_global_device_ids=true, to_apply=%add.2 | all-reduce | flops 1040 | bytes 8320
  120.6 0.1 reshape.51
  120.7 0.1 slice.8
  120.8 0.1 lt.44
  120.9 0.1 lt.39
  121.0 0.2 fusion.1
  121.2 0.0 all-gather.3.cloned.1.call-done
  121.2 2.5 %fusion = f32[65]{0:T(128)S(1)} fusion(bf16[1024,1024]{1,0:T(8,128)(2,1)} %all-gather.3.cloned.1.call-done, s32[1024]{0:T(1024)S(1)} %lt.39, s32[65]{0:T(128)S(1)} %multiply_bitcast_fusion.1, s32[65]{0:T(128)S(1)} %get-tuple-element.10, bf16[63,1024]{1,0:T(8,128)(2,1)S(1)} %fusion.3, bf16[2,1024]{1,0:T(2,128)(2,1)S(1)} %constant_dynamic-slice_fusion), kind=kOutput, calls=%fused_computation.1 | convolution fusion | flops 136913856 | bytes 2235148 | tf_op jit(solution)/shard_map/dot_general | solution.py:485
  123.7 0.5 compare_select_fusion
  (10 shorter events, 0.2 us)
Async XLA Ops:
  6.5 4.5 %copy-start.2 = (s32[4]{0:T(128)S(1)}, s32[4]{0:T(128)}, u32[]{:S(2)}) copy-start(s32[4]{0:T(128)} %len_ref.1) | copy-start | bytes 52
  6.5 4.5 %copy-start.1 = (bf16[512,256]{1,0:T(8,128)(2,1)S(1)}, bf16[512,256]{1,0:T(8,128)(2,1)}, u32[]{:S(2)}) copy-start(bf16[512,256]{1,0:T(8,128)(2,1)} %wo_ref.1) | copy-start | bytes 786436
  6.5 114.6 %all-gather.3.cloned.1.call-start = ((), (), s32[]{:S(2)}) async-start(), calls=%async_computation | async-start | bytes 2228224 | tf_op jit(solution)/shard_map/all_gather | solution.py:467
  11.1 79.7 %copy-start = (bf16[2048,256]{1,0:T(8,128)(2,1)S(1)}, bf16[2048,256]{1,0:T(8,128)(2,1)}, u32[]{:S(2)}) copy-start(bf16[2048,256]{1,0:T(8,128)(2,1)} %w_ref.1) | copy-start | bytes 3145732
  90.5 15.2 %copy-start.5 = (u32[32]{0:T(128)S(1)}, u32[32]{0:T(128)}, u32[]{:S(2)}) copy-start(u32[32]{0:T(128)} %constant.47) | copy-start | bytes 388
  90.5 16.4 %copy-start.3 = (s32[65]{0:T(128)S(1)}, s32[65]{0:T(128)}, u32[]{:S(2)}) copy-start(s32[65]{0:T(128)} %param.17) | copy-start | bytes 784
  90.5 16.4 %copy-start.4 = (s32[65,1]{0,1:T(1,128)S(1)}, s32[65,1]{0,1:T(1,128)}, u32[]{:S(2)}) copy-start(s32[65,1]{0,1:T(1,128)} %param.16) | copy-start | bytes 784
Sparse Core Ops, SparseCore 0:
  9.5 47.8 all-gather.2

commit v2 on v1

--- a/solution.py
+++ b/solution.py
@@ -245,7 +245,7 @@
                 scores = jnp.where(visible, scores, -jnp.inf)
                 weights = jnp.exp(scores - jnp.max(scores, axis=1, keepdims=True))
                 total = jnp.sum(weights, axis=1, keepdims=True)
-                weights = (weights / total).astype(jnp.bfloat16)
+                weights = (weights * (1.0 / total)).astype(jnp.bfloat16)
                 made.append(jnp.dot(weights, values, preferred_element_type=jnp.float32))
             context = jnp.where(lanes, made[0], made[1]).astype(jnp.bfloat16)
             c_buf[my_mp, doc, :, pair * LANES:(pair + 1) * LANES] = context
@@ -355,7 +355,10 @@
     )(lengths, hidden, w_qkv, w_out, w_up)
 
 
-def pool_kernel(n, mps, reps, act_ref, res_ref, w_ref, out_ref, a_buf, r_buf, a_send, a_recv, r_send, r_recv, p_send, p_recv):
+def pool_kernel(
+    n, mps, reps, act_ref, res_ref, w_ref, key_ref, out_ref, keys_ref,
+    a_buf, r_buf, a_send, a_recv, r_send, r_recv, p_send, p_recv, k_send, k_recv,
+):
     me, my_mp, rep = lax.axis_index("dp"), lax.axis_index("mp"), lax.axis_index("rep")
     count = n * mps * reps
     place = (me * mps + my_mp) * reps + rep
@@ -391,6 +394,20 @@
         return carry
 
     lax.fori_loop(1, n, give, 0)
+
+    def key_copy(source, target):
+        return pltpu.make_async_remote_copy(
+            src_ref=keys_ref.at[source], dst_ref=keys_ref.at[source], send_sem=k_send.at[target],
+            recv_sem=k_recv.at[source], device_id=at(target), device_id_type=MESH,
+        )
+
+    keys_ref[place] = key_ref[...]
+
+    def tell(k, carry):
+        key_copy(place, lax.rem(place + k, count)).start()
+        return carry
+
+    lax.fori_loop(1, count, tell, 0)
     a_buf[me] = act_ref[...]
     r_buf[me] = res_ref[me]
 
@@ -424,12 +441,13 @@
     def collect(k, carry):
         source = lax.rem(place + k, count)
         part_copy(source, source).wait()
+        key_copy(source, source).wait()
         return carry
 
     lax.fori_loop(1, count, collect, 0)
 
 
-def pool(acts, rest, w_down):
+def pool(acts, rest, w_down, key):
     n, mps, reps = lax.axis_size("dp"), lax.axis_size("mp"), lax.axis_size("rep")
     docs = acts.shape[0]
     count = n * mps * reps
@@ -437,18 +455,21 @@
     dma = pltpu.SemaphoreType.DMA
     return pl.pallas_call(
         functools.partial(pool_kernel, n, mps, reps),
-        out_shape=jax.ShapeDtypeStruct((count, n * docs, w_down.shape[1]), jnp.float32),
-        in_specs=[whole] * 3,
-        out_specs=whole,
+        out_shape=(
+            jax.ShapeDtypeStruct((count, n * docs, w_down.shape[1]), jnp.float32),
+            jax.ShapeDtypeStruct((count,) + key.shape, jnp.int32),
+        ),
+        in_specs=[whole] * 4,
+        out_specs=(whole, whole),
         scratch_shapes=[
             pltpu.VMEM((n,) + acts.shape, jnp.float32),
             pltpu.VMEM(rest.shape, jnp.float32),
-            dma((n,)), dma((n,)), dma((n,)), dma((n,)), dma((count,)), dma((count,)),
+            dma((n,)), dma((n,)), dma((n,)), dma((n,)), dma((count,)), dma((count,)), dma((count,)), dma((count,)),
         ],
         compiler_params=pltpu.CompilerParams(
             collective_id=1, has_side_effects=True, vmem_limit_bytes=52 * 1024 * 1024
         ),
-    )(acts, rest, w_down)
+    )(acts, rest, w_down, key)
 
 
 def shards(hidden_in, doc_lengths, w_qkv, w_out, w_up, w_down, stored_embed, doc_labels, doc_order):
@@ -467,14 +488,15 @@
     all_stored = lax.all_gather(
         jnp.pad(stored_units, ((0, spare), (0, 0))), ("dp", "mp", "rep"), axis=0, tiled=True
     )
-    keys = lax.all_gather(own_key, ("dp", "mp", "rep"), axis=0, tiled=False)
-    stored_keys = jnp.pad(keys[:, new_count:], ((0, 0), (0, spare)), constant_values=-1)
 
     acts, rest = encode(doc_lengths, hidden_in, w_qkv.reshape(w_qkv.shape[0], -1), w_out, w_up)
     scale = 1.0 / doc_lengths[:, None].astype(jnp.float32)
     acts = acts[:, 0] * scale
     rest = (rest[:, 0] * scale).reshape(docs, n, width // n).transpose(1, 0, 2)
-    parts = pool(acts, rest, w_down)
+    sent_key = jnp.pad(own_key, (0, -rows % LANES))[None]
+    parts, keys = pool(acts, rest, w_down, sent_key)
+    keys = keys[:, 0, :rows]
+    stored_keys = jnp.pad(keys[:, new_count:], ((0, 0), (0, spare)), constant_values=-1)
     pooled = jnp.sum(parts.reshape(n, mps, reps, n, docs, width // n), axis=1)
     pooled = pooled.transpose(2, 1, 3, 0, 4).reshape(n, reps, mps, new_count, width)
     new_units = unit_rows(pooled).transpose(0, 2, 1, 3, 4).reshape(blocks * new_count, width)

time: 131 us -> 117 us (0.89)
  blocking collectives: 13.5 us -> 0 us
    unnamed x1 -> x0, blocking collectives: 13.5 us -> none
    pallas_call x1, Pallas kernels: 14 us -> 15.6 us  [pool(): pl.pallas_call(functools.partial(pool_kernel, n, mps, reps), out_shape=(j...]
  transfers between devices with their start and end apart: 1 -> 1, of which waited for: 0 -> 0; matrix products, arithmetic and copies ran while one was open for 3% -> 3% of each run, Pallas kernels for 71% -> 81%
where the time goes in v2:
time: 117 us
  Pallas kernels  94.4 us (81%)
  between operations  13.6 us (12%)
  local copies, waits for them, and re-layouts  3.19 us (3%)
  other arithmetic  3.12 us (3%)
  matrix products  2.66 us (2%)
    pallas_call x1, Pallas kernels, encode(): pl.pallas_call(functools.partial(encode_kernel, n, mps, splits), out_shap...  78.8 us
    pallas_call x1, Pallas kernels, pool(): pl.pallas_call(functools.partial(pool_kernel, n, mps, reps), out_shape=(j...  15.6 us
    dot_general x2, matrix products, best_of(): lax.dot_general(own_rows, units, (((1,), (1,)), ((), ())), preferred_elem...  2.66 us
  transfers between devices with their start and end apart: 1, of which 0 were waited for; matrix products, arithmetic and copies ran while one was open for 3% of the time, Pallas kernels for 81%

profile of v2, /device:TPU:0, one launch (start us, length us, event | category | flops | bytes accessed | tf_op | source)
XLA Modules:
  0.0 117.0 jit_solution(9140336212029915263)
XLA Ops:
  6.5 0.0 copy-start.2
  6.5 0.0 copy-start.1
  6.5 0.0 all-gather.2.cloned.1.call-start
  6.5 1.1 fusion.2
  7.6 1.0 fusion.3
  8.6 0.7 pad.14
  9.3 0.0 all-gather.2.cloned.1.call-update
  9.3 1.4 %copy.29 = bf16[256,3,512]{0,2,1:T(8,128)(2,1)S(1)} copy(bf16[256,3,512]{2,0,1:T(8,128)(2,1)} %param.11) | data formatting | bytes 1572864 | tf_op args[2]
  10.7 0.3 copy.30.wq_ref
  11.0 0.0 copy-done.2
  11.0 0.0 copy-done.1
  11.0 0.0 copy-start.3
  11.1 0.0 copy-start.4
  11.1 0.0 copy-start
  11.1 78.8 %shard_map.91 = (f32[4,1,2048]{2,1,0:T(1,128)S(1)}, f32[4,1,1024]{2,1,0:T(1,128)S(1)}) custom-call(s32[4]{0:T(128)S(1)} %copy-done.2, bf16[4,256,1024]{2,1,0:T(8,128)(2,1)} %hid_ref.1, bf16[256,1536]{1,0:T(8,128)(2,1)S(1)} %copy.30.wq_ref, bf16[512,256]{1,0:T(8,128)(2,1)S(1)} %copy-done.1, bf16[256,2048]{1,0:T(8,128)(2,1)} %wu_ref.1), custom_call_target="tpu_custom_call" | custom-call | flops 12000000000 | bytes 100000000 | tf_op jit(solution)/shard_map/pallas_call | solution.py:328
  90.0 0.0 copy-done.3
  90.0 0.0 copy-done.4
  90.0 0.1 multiply_bitcast_fusion.res_ref
  90.1 0.1 bitcast_multiply_fusion.act_ref
  90.2 0.0 copy-done
  90.2 15.6 %shard_map.92 = (f32[16,16,256]{2,1,0:T(8,128)S(1)}, s32[16,1,128]{2,1,0:T(1,128)S(1)}) custom-call(f32[4,2048]{1,0:T(4,128)S(1)} %bitcast_multiply_fusion.act_ref, f32[4,4,256]{2,1,0:T(4,128)S(1)} %multiply_bitcast_fusion.res_ref, bf16[2048,256]{1,0:T(8,128)(2,1)S(1)} %copy-done, s32[1,128]{1,0:T(1,128)S(1)} %pad_bitcast_fusion.key_ref), custom_call_target="tpu_custom_call" | custom-call | tf_op jit(solution)/shard_map/pallas_call | solution.py:456
  105.8 0.1 reshape.48
  105.8 0.1 reduce_sum.27
  105.9 0.1 copy.32
  106.0 0.1 reshape.49
  106.1 0.1 multiply_reduce_fusion
  106.3 0.1 copy.35
  106.4 0.1 copy.36
  106.5 0.1 fusion.4
  106.7 0.1 slice.12
  106.8 0.1 lt.44
  106.9 0.1 lt.39
  107.0 0.2 fusion.1
  107.2 0.0 all-gather.2.cloned.1.call-done
  107.2 2.5 %fusion = f32[65]{0:T(128)S(1)} fusion(bf16[1024,1024]{1,0:T(8,128)(2,1)} %all-gather.2.cloned.1.call-done, s32[1024]{0:T(1024)S(1)} %lt.39, s32[65]{0:T(128)S(1)} %multiply_bitcast_fusion.1, s32[65]{0:T(128)S(1)} %fusion.7, bf16[63,1024]{1,0:T(8,128)(2,1)S(1)} %fusion.3, bf16[2,1024]{1,0:T(2,128)(2,1)S(1)} %constant_dynamic-slice_fusion), kind=kOutput, calls=%fused_computation.1 | convolution fusion | flops 136913856 | bytes 2235148 | tf_op jit(solution)/shard_map/dot_general | solution.py:507
  109.7 0.5 compare_select_fusion
  (11 shorter events, 0.2 us)
Async XLA Ops:
  6.5 4.5 %copy-start.2 = (s32[4]{0:T(128)S(1)}, s32[4]{0:T(128)}, u32[]{:S(2)}) copy-start(s32[4]{0:T(128)} %len_ref.1) | copy-start | bytes 52
  6.5 4.5 %copy-start.1 = (bf16[512,256]{1,0:T(8,128)(2,1)S(1)}, bf16[512,256]{1,0:T(8,128)(2,1)}, u32[]{:S(2)}) copy-start(bf16[512,256]{1,0:T(8,128)(2,1)} %wo_ref.1) | copy-start | bytes 786436
  6.5 100.6 %all-gather.2.cloned.1.call-start = ((), (), s32[]{:S(2)}) async-start(), calls=%async_computation | async-start | bytes 2228224 | tf_op jit(solution)/shard_map/all_gather | solution.py:488
  11.0 78.9 %copy-start.3 = (s32[65]{0:T(128)S(1)}, s32[65]{0:T(128)}, u32[]{:S(2)}) copy-start(s32[65]{0:T(128)} %param.17) | copy-start | bytes 784
  11.1 78.9 %copy-start.4 = (s32[65,1]{0,1:T(1,128)S(1)}, s32[65,1]{0,1:T(1,128)}, u32[]{:S(2)}) copy-start(s32[65,1]{0,1:T(1,128)} %param.16) | copy-start | bytes 784
  11.1 79.1 %copy-start = (bf16[2048,256]{1,0:T(8,128)(2,1)S(1)}, bf16[2048,256]{1,0:T(8,128)(2,1)}, u32[]{:S(2)}) copy-start(bf16[2048,256]{1,0:T(8,128)(2,1)} %w_ref.1) | copy-start | bytes 3145732
Sparse Core Ops, SparseCore 0:
  9.5 47.6 all-gather.1

commit v3 on v2

--- a/solution.py
+++ b/solution.py
@@ -214,8 +214,12 @@
     def _():
         pl.semaphore_wait(barrier, 2 + mps)
 
+    own(1)
     own(0)
-    own(1)
+    steps(1, 1, n)
+    finish(1)
+    for k in range(1, mps):
+        out_copy(my_mp, k).start()
     steps(0, 1, n - 1)
     own(2)
     steps(0, n - 1, n)
@@ -252,13 +256,6 @@
 
         for k in range(1, mps):
             context_copy(my_mp, k, doc).start()
-
-        @pl.when(doc == 0)
-        def _():
-            steps(1, 1, n)
-            finish(1)
-            for k in range(1, mps):
-                out_copy(my_mp, k).start()
 
         for k in range(3):
             @pl.when(doc == min(k + 1, docs - 1))

time: 117 us -> 119 us (1.017)
  Pallas kernels: 94.4 us -> 96 us
    pallas_call x1, Pallas kernels: 78.8 us -> 80.9 us  [encode(): pl.pallas_call(functools.partial(encode_kernel, n, mps, splits), out_shap...]
where the time goes in v3:
time: 119 us
  Pallas kernels  96 us (81%)
  between operations  13.6 us (11%)
  local copies, waits for them, and re-layouts  3.19 us (3%)
  other arithmetic  3.12 us (3%)
  matrix products  2.66 us (2%)
    pallas_call x1, Pallas kernels, encode(): pl.pallas_call(functools.partial(encode_kernel, n, mps, splits), out_shap...  80.9 us
    pallas_call x1, Pallas kernels, pool(): pl.pallas_call(functools.partial(pool_kernel, n, mps, reps), out_shape=(j...  15 us
    dot_general x2, matrix products, best_of(): lax.dot_general(own_rows, units, (((1,), (1,)), ((), ())), preferred_elem...  2.66 us
  transfers between devices with their start and end apart: 1, of which 0 were waited for; matrix products, arithmetic and copies ran while one was open for 3% of the time, Pallas kernels for 81%

profile of v3, /device:TPU:0, one launch (start us, length us, event | category | flops | bytes accessed | tf_op | source)
XLA Modules:
  0.0 118.6 jit_solution(12484858271686073866)
XLA Ops:
  6.5 0.0 copy-start.2
  6.5 0.0 copy-start.1
  6.5 0.0 all-gather.2.cloned.1.call-start
  6.5 1.1 fusion.2
  7.6 1.0 fusion.3
  8.6 0.7 pad.14
  9.3 0.0 all-gather.2.cloned.1.call-update
  9.3 1.4 %copy.29 = bf16[256,3,512]{0,2,1:T(8,128)(2,1)S(1)} copy(bf16[256,3,512]{2,0,1:T(8,128)(2,1)} %param.11) | data formatting | bytes 1572864 | tf_op args[2]
  10.7 0.3 copy.30.wq_ref
  11.0 0.0 copy-done.2
  11.0 0.0 copy-done.1
  11.0 0.0 copy-start.3
  11.1 0.0 copy-start.4
  11.1 0.0 copy-start
  11.1 80.9 %shard_map.91 = (f32[4,1,2048]{2,1,0:T(1,128)S(1)}, f32[4,1,1024]{2,1,0:T(1,128)S(1)}) custom-call(s32[4]{0:T(128)S(1)} %copy-done.2, bf16[4,256,1024]{2,1,0:T(8,128)(2,1)} %hid_ref.1, bf16[256,1536]{1,0:T(8,128)(2,1)S(1)} %copy.30.wq_ref, bf16[512,256]{1,0:T(8,128)(2,1)S(1)} %copy-done.1, bf16[256,2048]{1,0:T(8,128)(2,1)} %wu_ref.1), custom_call_target="tpu_custom_call" | custom-call | flops 12000000000 | bytes 100000000 | tf_op jit(solution)/shard_map/pallas_call | solution.py:325
  92.0 0.0 copy-done.3
  92.1 0.0 copy-done.4
  92.1 0.1 multiply_bitcast_fusion.res_ref
  92.2 0.1 bitcast_multiply_fusion.act_ref
  92.3 0.0 copy-done
  92.3 15.0 %shard_map.92 = (f32[16,16,256]{2,1,0:T(8,128)S(1)}, s32[16,1,128]{2,1,0:T(1,128)S(1)}) custom-call(f32[4,2048]{1,0:T(4,128)S(1)} %bitcast_multiply_fusion.act_ref, f32[4,4,256]{2,1,0:T(4,128)S(1)} %multiply_bitcast_fusion.res_ref, bf16[2048,256]{1,0:T(8,128)(2,1)S(1)} %copy-done, s32[1,128]{1,0:T(1,128)S(1)} %pad_bitcast_fusion.key_ref), custom_call_target="tpu_custom_call" | custom-call | tf_op jit(solution)/shard_map/pallas_call | solution.py:453
  107.3 0.1 reshape.48
  107.4 0.1 reduce_sum.27
  107.5 0.1 copy.32
  107.6 0.1 reshape.49
  107.7 0.1 multiply_reduce_fusion
  107.8 0.1 copy.35
  107.9 0.1 copy.36
  108.0 0.1 fusion.4
  108.2 0.1 slice.12
  108.3 0.1 lt.44
  108.4 0.1 lt.39
  108.5 0.2 fusion.1
  108.7 0.0 all-gather.2.cloned.1.call-done
  108.7 2.5 %fusion = f32[65]{0:T(128)S(1)} fusion(bf16[1024,1024]{1,0:T(8,128)(2,1)} %all-gather.2.cloned.1.call-done, s32[1024]{0:T(1024)S(1)} %lt.39, s32[65]{0:T(128)S(1)} %multiply_bitcast_fusion.1, s32[65]{0:T(128)S(1)} %fusion.7, bf16[63,1024]{1,0:T(8,128)(2,1)S(1)} %fusion.3, bf16[2,1024]{1,0:T(2,128)(2,1)S(1)} %constant_dynamic-slice_fusion), kind=kOutput, calls=%fused_computation.1 | convolution fusion | flops 136913856 | bytes 2235148 | tf_op jit(solution)/shard_map/dot_general | solution.py:504
  111.2 0.5 compare_select_fusion
  (11 shorter events, 0.2 us)
Async XLA Ops:
  6.5 4.5 %copy-start.2 = (s32[4]{0:T(128)S(1)}, s32[4]{0:T(128)}, u32[]{:S(2)}) copy-start(s32[4]{0:T(128)} %len_ref.1) | copy-start | bytes 52
  6.5 4.5 %copy-start.1 = (bf16[512,256]{1,0:T(8,128)(2,1)S(1)}, bf16[512,256]{1,0:T(8,128)(2,1)}, u32[]{:S(2)}) copy-start(bf16[512,256]{1,0:T(8,128)(2,1)} %wo_ref.1) | copy-start | bytes 786436
  6.5 102.2 %all-gather.2.cloned.1.call-start = ((), (), s32[]{:S(2)}) async-start(), calls=%async_computation | async-start | bytes 2228224 | tf_op jit(solution)/shard_map/all_gather | solution.py:485
  11.0 81.0 %copy-start.3 = (s32[65]{0:T(128)S(1)}, s32[65]{0:T(128)}, u32[]{:S(2)}) copy-start(s32[65]{0:T(128)} %param.17) | copy-start | bytes 784
  11.1 81.0 %copy-start.4 = (s32[65,1]{0,1:T(1,128)S(1)}, s32[65,1]{0,1:T(1,128)}, u32[]{:S(2)}) copy-start(s32[65,1]{0,1:T(1,128)} %param.16) | copy-start | bytes 784
  11.1 81.2 %copy-start = (bf16[2048,256]{1,0:T(8,128)(2,1)S(1)}, bf16[2048,256]{1,0:T(8,128)(2,1)}, u32[]{:S(2)}) copy-start(bf16[2048,256]{1,0:T(8,128)(2,1)} %w_ref.1) | copy-start | bytes 3145732
Sparse Core Ops, SparseCore 0:
  9.5 50.1 all-gather.1
